TPU v7x, 128 devices: a whole 4x4x4 slice. The times are simulated.
128 devices in a mesh: gen: 8 (over y, core), voc: 16 (over x, z).
Axes of the slice: x: 4, y: 4, z: 4, core: 2. Of those that a mesh axis runs over, the one named last changes fastest.
Arguments:
- features: bfloat16 [8192, 24, 128], P(('gen', 'voc')), may hold values from -6 to 6
- target: int32 [8192], P(('gen', 'voc')), may hold values from -1 to 511, as said below
- extents: int32 [8192, 3], P(('gen', 'voc')), may hold values from 0 to 24, as said below
- w_pre: bfloat16 [896, 1536], replicated, may hold values from -0.1875 to 0.1875
- biases: float32 [1536], replicated, may hold values from -1.5 to 1.5
- snake_params: float32 [2, 1536], replicated, may hold values from 0.4 to 2.5
- w_up: bfloat16 [1536, 6144], replicated, may hold values from -0.109375 to 0.109375
- up_bias: float32 [768], replicated, may hold values from -1.5 to 1.5
Outputs:
- waves: bfloat16 [8192, 96, 768], P(('gen', 'voc'))
Inputs may be any that keep to these rules, and one draw needn't show every extreme that they name: Within each gen group every (voc index, slot) pair target[i] = voc index * 32 + slot is named by exactly one generator slot; -1 marks an empty generator slot. No generator device names one vocoder device more than 4 times, and in every group some device does so exactly 4 times for each vocoder device. `extents`: column 0 is 24 except for the last segment of an utterance; columns 1 and 2 are 0 where the stream neighbour belongs to another utterance and equal its column 0 otherwise; all zero for empty slots.
All inputs are finite; a program needn't handle non-finite values.
Results may differ from a plain program's by a relative error of at most 0.0048.
Values may be sent and summed in bfloat16 or wider, within the bound.
No kernel may reach another device: no remote copies, remote signals or barrier semaphores. Data moves between devices by JAX's collectives and lax.ppermute only.
A program may use at most 192 MiB of HBM per device.

v0:
```python
import functools

import jax
import jax.numpy as jnp
from jax import lax
from jax.experimental import pallas as pl
from jax.experimental.pallas import tpu as pltpu
from jax.sharding import PartitionSpec as P

UP = 4
KPRE = 7
RIM = 4
CAP = 4
LANES = 128
STEP = 256

SIN2 = (9.869604311707747, -32.46967117172015, 42.72719633651888, -30.101465841328583, 13.050098920339147, -3.3565926218240247)


def copy_of(src, dst, sem):
    return pltpu.make_async_copy(src, dst, sem)


def vocode_kernel(starts, frames, rims, plan, features, *rest):
    if rims:
        home, w_pre, w_up, vectors, _, out = rest[:6]
        scratch = rest[6:]
    else:
        home = None
        w_pre, w_up, vectors, out = rest[:4]
        scratch = rest[4:]
    (wp, wu, win, msk, taps, acts, rows32, stage, zeros, slots, ranks, counts, w_sem, out_sem, zero_sem) = scratch
    pieces = len(starts)
    act_rows = frames + 2
    win_rows = frames + 8
    seg = features.shape[1]
    channels = wp.shape[1]
    width = wu.shape[1] // (2 * UP)
    n_slots = features.shape[0]
    span = UP * frames
    pitch = span + 8
    parts = width // STEP
    tiles = STEP // LANES

    phases = tuple((r + UP // 2, r + UP + UP // 2 if r < UP // 2 else r - UP // 2) for r in range(UP))

    def load_taps(n, start):
        for tap in sum(phases, ()):
            cols = pl.ds(pl.multiple_of(tap * width + n * STEP, STEP), STEP)
            copy = copy_of(w_up.at[:, cols], wu.at[:, cols], w_sem.at[n, tap])
            copy.start() if start else copy.wait()

    def load_pre(start):
        copy = copy_of(w_pre, wp, w_sem.at[parts, 0])
        copy.start() if start else copy.wait()

    load_pre(True)
    for n in range(parts):
        load_taps(n, True)
    for v in range(17):
        counts[v] = 0
    slots[0] = 0
    ranks[0] = 0

    def scan(i, found):
        code = plan[i]
        used = code >= 0
        slots[found] = i
        if rims:
            worker = jnp.where(used, lax.shift_right_logical(code, 5), 16)
            rank = counts[worker]
            ranks[found] = rank
            counts[worker] = rank + 1
        return found + used.astype(jnp.int32)

    found = lax.fori_loop(0, n_slots, scan, jnp.int32(0), unroll=8)

    cell = lax.broadcasted_iota(jnp.int32, (seg, LANES), 0)
    rim_cell = lax.broadcasted_iota(jnp.int32, (2 * RIM, LANES), 0)

    def fill(block, b):
        c = jnp.minimum(b, found - 1)
        slot = slots[c]
        own = (cell < plan[n_slots + slot * 3]).astype(jnp.float32)
        values = features[slot].astype(jnp.float32) * own
        if not rims:
            win[0, pl.ds(b, seg, stride=block), :] = values
            msk[0, pl.ds(b, seg, stride=block), :] = own
        else:
            at = RIM * block + b
            inner = win_rows - RIM
            win[0, pl.ds(at, inner, stride=block), :] = values[:inner]
            msk[0, pl.ds(at, inner, stride=block), :] = own[:inner]
            win[1, pl.ds(b, inner, stride=block), :] = values[seg - inner :]
            msk[1, pl.ds(b, inner, stride=block), :] = own[seg - inner :]
            worker = lax.shift_right_logical(plan[slot], 5)
            rank = ranks[c]
            before_ok = (rim_cell - RIM + seg - RIM < plan[n_slots + slot * 3 + 1]).astype(jnp.float32)
            after_ok = (rim_cell < plan[n_slots + slot * 3 + 2]).astype(jnp.float32)
            before = home[worker, rank].astype(jnp.float32) * before_ok
            after = home[(worker + 1) & 15, rank].astype(jnp.float32) * after_ok
            win[0, pl.ds(b, RIM, stride=block), :] = before[RIM:]
            msk[0, pl.ds(b, RIM, stride=block), :] = before_ok[RIM:]
            tail = inner * block + b
            win[1, pl.ds(tail, RIM, stride=block), :] = after[:RIM]
            msk[1, pl.ds(tail, RIM, stride=block), :] = after_ok[:RIM]

            def far(row, rows_from):
                code = (plan[slot] & 31).astype(jnp.float32) + 1.0

                def look(k, total):
                    codes = home[k, 2 * CAP].astype(jnp.float32)
                    for e in range(CAP):
                        entry = home[k, CAP + e].astype(jnp.float32)
                        total = total + jnp.where(codes[row + e : row + e + 1] == code, entry, 0.0)
                    return total

                total = lax.fori_loop(0, home.shape[0], look, jnp.zeros((2 * RIM, LANES), jnp.float32), unroll=2)
                return total[rows_from : rows_from + RIM]

            @pl.when(worker == 0)
            def _():
                win[0, pl.ds(b, RIM, stride=block), :] = far(0, 0) * before_ok[RIM:]

            @pl.when(worker == 15)
            def _():
                win[1, pl.ds(tail, RIM, stride=block), :] = far(CAP, RIM) * after_ok[:RIM]

    def run(block):
        rows = act_rows * block

        def fill_one(b, c):
            fill(block, b)
            return c

        lax.fori_loop(0, block, fill_one, 0, unroll=2)
        for p in range(pieces):
            for q in range(KPRE):
                taps[pl.ds(p * rows, rows), pl.ds(q * LANES, LANES)] = win[p, pl.ds(q * block, rows), :].astype(
                    jnp.bfloat16
                )

        load_pre(False)

        if not rims:
            zeros[...] = jnp.zeros_like(zeros)

            def clear(i, c):
                @pl.when(plan[i] < 0)
                def _():
                    copy_of(zeros, out.at[i], zero_sem.at[i]).start()

                return c

            lax.fori_loop(0, n_slots, clear, 0)

        def conv_chunk(n, c):
            def vector(i):
                return vectors[:, pl.ds(pl.multiple_of(i * channels + n * STEP, STEP), STEP)]

            cols = pl.ds(pl.multiple_of(n * STEP, STEP), STEP)
            bias = vector(0)
            scale = vector(1) * (1.0 / jnp.pi)
            inverse = 1.0 / vector(2)
            for p in range(pieces):
                sums = jnp.dot(taps[pl.ds(p * rows, rows), :], wp[:, cols], preferred_element_type=jnp.float32)
                mask = msk[p, pl.ds(3 * block, rows), :]
                hidden = jnp.concatenate([mask] * tiles, axis=1) * (sums + bias)
                turns = hidden * scale
                rest_of = turns - jnp.floor(turns + 0.5)
                u = rest_of * rest_of
                poly = SIN2[-1] * u + SIN2[-2]
                for coef in SIN2[-3::-1]:
                    poly = poly * u + coef
                acts[pl.ds(p * rows, rows), cols] = (hidden + u * poly * inverse).astype(jnp.bfloat16)
            return c

        lax.fori_loop(0, channels // STEP, conv_chunk, 0, unroll=2)

        def acts_from(shift):
            picked = [acts[pl.ds(p * rows + shift * block, frames * block), :] for p in range(pieces)]
            return picked[0] if pieces == 1 else jnp.concatenate(picked, axis=0)

        def up_part(n, c):
            load_taps(n, False)
            for r in range(UP):
                sums = vectors[:, pl.ds(pl.multiple_of(3 * channels + n * STEP, STEP), STEP)]
                for tap, shift in zip(phases[r], (1, 0 if r < UP // 2 else 2)):
                    cols = pl.ds(pl.multiple_of(tap * width + n * STEP, STEP), STEP)
                    sums = sums + jnp.dot(acts_from(shift), wu[:, cols], preferred_element_type=jnp.float32)
                for p in range(pieces):
                    for j in range(frames):
                        mask = msk[p, pl.ds((j + 4) * block, block), :]
                        here = (p * frames + j) * block
                        for half in range(tiles):
                            rows32[
                                n * tiles + half, pl.ds(p * block * pitch + UP * j + r, block, stride=pitch), :
                            ] = mask * sums[here : here + block, half * LANES : (half + 1) * LANES]
            return c

        lax.fori_loop(0, parts, up_part, 0)

        def send(b, c):
            for p in range(pieces):
                for n in range(width // LANES):
                    stage[p, b, :, n * LANES : (n + 1) * LANES] = rows32[
                        n, pl.ds(pl.multiple_of((p * block + b) * pitch, 8), span), :
                    ].astype(jnp.bfloat16)

            @pl.when(b < found)
            def _():
                for p in range(pieces):
                    copy_of(stage.at[p, b], out.at[slots[b], pl.ds(UP * starts[p], span)], out_sem.at[p, b]).start()

            return c

        lax.fori_loop(0, block, send, 0)

    for units in range(1, 5):

        @pl.when((found > 16 * (units - 1)) & (found <= 16 * units))
        def _(units=units):
            run(16 * units)

    @pl.when(found == 0)
    def _():
        load_pre(False)
        for n in range(parts):
            load_taps(n, False)
        if not rims:
            zeros[...] = jnp.zeros_like(zeros)

            def clear(i, c):
                copy_of(zeros, out.at[i], zero_sem.at[i]).start()
                return c

            lax.fori_loop(0, n_slots, clear, 0)

    def settle(b, c):
        for p in range(pieces):
            copy_of(stage.at[p, b], out.at[0, pl.ds(0, span)], out_sem.at[p, b]).wait()
        return c

    lax.fori_loop(0, found, settle, 0)

    if not rims:

        def cleared(i, c):
            @pl.when(plan[i] < 0)
            def _():
                copy_of(zeros, out.at[i], zero_sem.at[i]).wait()

            return c

        lax.fori_loop(0, n_slots, cleared, 0)


def vocode(starts, frames, home, waves, plan, features, w_pre, w_up, vectors):
    rims = home is not None
    pieces = len(starts)
    n_slots, seg, feat = features.shape
    channels = w_pre.shape[1]
    width = w_up.shape[1] // (2 * UP)
    span = UP * frames
    smem = pl.BlockSpec(memory_space=pltpu.SMEM)
    vmem = pl.BlockSpec(memory_space=pltpu.VMEM)
    hbm = pl.BlockSpec(memory_space=pl.ANY)
    operands = [plan, features]
    specs = [smem, vmem]
    if rims:
        operands.append(home)
        specs.append(vmem)
    operands += [w_pre, w_up, vectors]
    specs += [hbm, hbm, vmem]
    aliases = {}
    if rims:
        aliases = {len(operands): 0}
        operands.append(waves)
        specs.append(hbm)
    return pl.pallas_call(
        functools.partial(vocode_kernel, starts, frames, rims),
        out_shape=jax.ShapeDtypeStruct((n_slots, UP * seg, width), jnp.bfloat16),
        in_specs=specs,
        out_specs=hbm,
        input_output_aliases=aliases,
        scratch_shapes=[
            pltpu.VMEM(w_pre.shape, jnp.bfloat16),
            pltpu.VMEM(w_up.shape, jnp.bfloat16),
            pltpu.VMEM((pieces, (frames + 8) * n_slots, feat), jnp.float32),
            pltpu.VMEM((pieces, (frames + 8) * n_slots, feat), jnp.float32),
            pltpu.VMEM((pieces * (frames + 2) * n_slots, KPRE * feat), jnp.bfloat16),
            pltpu.VMEM((pieces * (frames + 2) * n_slots, channels), jnp.bfloat16),
            pltpu.VMEM((width // LANES, pieces * n_slots * (span + 8), LANES), jnp.float32),
            pltpu.VMEM((pieces, n_slots, span, width), jnp.bfloat16),
            pltpu.VMEM((16, LANES) if rims else (UP * seg, width), jnp.bfloat16),
            pltpu.SMEM((n_slots + 1,), jnp.int32),
            pltpu.SMEM((n_slots + 1,), jnp.int32),
            pltpu.SMEM((17,), jnp.int32),
            pltpu.SemaphoreType.DMA((width // STEP + 1, 2 * UP)),
            pltpu.SemaphoreType.DMA((pieces, n_slots)),
            pltpu.SemaphoreType.DMA((n_slots,)),
        ],
        compiler_params=pltpu.CompilerParams(vmem_limit_bytes=58 * 2**20),
        cost_estimate=pl.CostEstimate(
            flops=2 * 48 * pieces * frames * 2 * channels * UP * width,
            bytes_accessed=2 * (w_up.size + w_pre.size + 48 * pieces * span * width),
            transcendentals=0,
        ),
        name="edges" if rims else "inner",
    )(*operands)


def one_hot_rows(match, values):
    rows = jnp.dot(match.astype(jnp.bfloat16), values.reshape(values.shape[0], -1), preferred_element_type=jnp.float32)
    return rows.astype(jnp.bfloat16)


def packed(features, target):
    n_slots, seg, feat = features.shape
    used = target >= 0
    worker = jnp.where(used, target // 32, -1)
    order = jnp.arange(n_slots, dtype=jnp.int32)
    rank = jnp.sum(((worker[:, None] == worker[None, :]) & (order[:, None] < order[None, :])).astype(jnp.int32), axis=0)
    slot = target % 32 + 1

    def sorted_rows(worker_of, values):
        row = jnp.where(used, worker_of * CAP + rank, -1)
        select = row[None, :] == jnp.arange(16 * CAP, dtype=jnp.int32)[:, None]
        code = jnp.sum(jnp.where(select, slot[None, :], 0), axis=1).astype(jnp.bfloat16)
        return one_hot_rows(select, values).reshape(16, CAP, RIM, feat), code.reshape(16, CAP)

    heads, head_code = sorted_rows(worker, features[:, :RIM])
    tails, tail_code = sorted_rows((worker + 1) % 16, features[:, seg - RIM :])
    codes = jnp.concatenate([tail_code, head_code], axis=1)
    codes = jnp.broadcast_to(codes[:, None, :, None], (16, 1, 2 * CAP, feat))
    return jnp.concatenate([jnp.concatenate([tails, heads], axis=2), codes], axis=1)


def swapped(got):
    def codes(first):
        return got[:, CAP, first : first + CAP, 0].astype(jnp.int32).reshape(-1)

    def entries(first):
        return got[:, :CAP, first : first + RIM].reshape(got.shape[0] * CAP, -1)

    tail_code, head_code = codes(0), codes(RIM)
    match = (tail_code[:, None] == head_code[None, :]) & (tail_code[:, None] > 0)
    shape = (got.shape[0], CAP, RIM, got.shape[3])
    heads = one_hot_rows(match, entries(RIM)).reshape(shape)
    tails = one_hot_rows(match.T, entries(0)).reshape(shape)
    return jnp.concatenate([heads, tails], axis=2)


def from_groups(own):
    gen, count = lax.axis_index("gen"), lax.axis_size("gen")
    lower = lax.ppermute(own, "gen", [(g, (g + 1) % count) for g in range(count)])[:, :RIM]
    upper = lax.ppermute(own, "gen", [(g, (g - 1) % count) for g in range(count)])[:, RIM:]
    tail_code, head_code = lower[CAP].astype(jnp.float32), upper[CAP].astype(jnp.float32)
    stepped = jnp.where(tail_code == 32, 1.0, tail_code + 1)
    tail_code = jnp.where((gen == 0) & (tail_code > 0), stepped, tail_code)
    stepped = jnp.where(head_code == 1, 32.0, head_code - 1)
    head_code = jnp.where((gen == count - 1) & (head_code > 0), stepped, head_code)
    codes = jnp.concatenate([tail_code, head_code], axis=0).astype(own.dtype)
    return jnp.concatenate([jnp.concatenate([lower[:CAP], upper[:CAP]], axis=1), codes[None]], axis=0)


def on_device(features, target, extents, w_pre, biases, snake_params, w_up, up_bias):
    rims = packed(features, target)
    plan = jnp.concatenate([target, extents.reshape(-1)])
    far = from_groups(lax.optimization_barrier((rims[0], plan))[0])
    got = lax.all_to_all(rims, "voc", split_axis=0, concat_axis=0, tiled=True)
    back = jnp.concatenate([swapped(got), jnp.broadcast_to(far, rims.shape)], axis=1)
    home = lax.all_to_all(back, "voc", split_axis=0, concat_axis=0, tiled=True)
    vectors = jnp.concatenate([biases, snake_params.reshape(-1), up_bias])[None, :]
    rest = (plan, features, w_pre, w_up, vectors)
    waves = vocode((RIM,), 16, None, None, *rest)
    return vocode((0, 20), 4, home, waves, *rest)


def solution(mesh):
    split = P(("gen", "voc"))
    return jax.shard_map(
        on_device,
        mesh=mesh,
        in_specs=(split, split, split, P(), P(), P(), P(), P()),
        out_specs=split,
        check_vma=False,
    )
```

profile of v0, /device:TPU:36, one launch (start us, length us, event | category | flops | bytes accessed | tf_op | source)
XLA Modules:
  0.0 80.9 jit_solution(12659187026450551809)
XLA Ops:
  0.0 0.7 fusion.28
  0.7 0.1 convert_reduce_fusion.2
  0.8 0.7 add_select_fusion
  1.4 0.1 select_reduce_fusion.1
  1.6 0.1 convert_element_type.79
  1.7 0.1 convert_element_type.77
  1.8 1.0 %fusion.29 = (bf16[64,4,128]{2,1,0:T(4,128)(2,1)S(1)}, bf16[64,4,128]{2,1,0:T(4,128)(2,1)S(1)}) fusion(bf16[64,24,128]{2,1,0:T(8,128)(2,1)} %features.3), kind=kLoop, calls=%fused_computation.68 | loop fusion | bytes 262144 | tf_op jit(solution)/shard_map/slice | solution.py:333
  2.8 0.1 convolution_convert_fusion.3
  3.0 0.1 convolution_convert_fusion.2
  3.2 0.1 pad_maximum_fusion.3
  3.2 0.1 broadcast_in_dim.50
  3.3 0.7 pad_maximum_fusion.1
  4.1 7.8 %all-to-all-start = ((bf16[16,5,8,128]{3,2,1,0:T(8,128)(2,1)}), bf16[16,5,8,128]{3,2,1,0:T(8,128)(2,1)S(1)}, u32[]{:S(2)}, u32[]{:S(2)}) async-start(bf16[16,5,8,128]{3,2,1,0:T(8,128)(2,1)} %pad_maximum_fusion.1), calls=%async_computation | async-start | bytes 327680 | tf_op jit(solution)/shard_map/all_to_all | solution.py:371
  11.9 0.7 slice_bitcast_fusion
  12.6 0.8 copy.14
  13.4 0.1 reshape.88
  13.6 1.3 %pad_add_fusion.plan = s32[256]{0:T(256)} fusion(s32[192]{0:T(256)S(1)} %reshape.88, s32[64]{0:T(128)} %param.9), kind=kLoop, calls=%fused_computation.58 | loop fusion | flops 256 | bytes 2048 | tf_op jit(solution)/shard_map/concatenate | solution.py:369
  14.9 1.9 %collective-permute-start.1 = (bf16[5,8,128]{2,1,0:T(8,128)(2,1)S(1)}, bf16[5,8,128]{2,1,0:T(8,128)(2,1)S(1)}, u32[]{:S(2)}, u32[]{:S(2)}) collective-permute-start(bf16[5,8,128]{2,1,0:T(8,128)(2,1)S(1)} %slice_bitcast_fusion), channel_id=1, source_target_pairs={{0,112},{16,0},{32,16},{48,32},{64,48},{80,64},{96,80},{112,96},{1... | collective-permute-start | bytes 30728 | tf_op jit(solution)/shard_map/ppermute | solution.py:357
  16.8 0.0 collective-permute-start
  16.8 0.7 reshape.97
  17.5 0.7 pad_maximum_fusion.2
  18.2 0.6 broadcast_in_dim.53.rest_2_.rest_3_
  18.8 0.0 collective-permute-done.1
  18.9 2.2 %collective-permute-done = bf16[5,8,128]{2,1,0:T(8,128)(2,1)S(1)} collective-permute-done((bf16[5,8,128]{2,1,0:T(8,128)(2,1)S(1)}, bf16[5,8,128]{2,1,0:T(8,128)(2,1)S(1)}, u32[]{:S(2)}, u32[]{:S(2)}) %collective-permute-start) | collective-permute-done | bytes 10272 | tf_op jit(solution)/shard_map/ppermute | solution.py:356
  21.1 0.0 all-to-all-done
  21.1 0.6 convert_reduce_fusion.1
  21.8 0.1 reshape.98
  21.9 0.1 reshape.99
  22.0 0.3 convolution_convert_fusion
  22.3 0.2 convolution_convert_fusion.1
  22.6 0.8 pad_maximum_fusion
  23.4 7.2 %all-to-all-start.1 = ((bf16[16,9,8,128]{3,2,1,0:T(8,128)(2,1)}), bf16[16,9,8,128]{3,2,1,0:T(8,128)(2,1)S(1)}, u32[]{:S(2)}, u32[]{:S(2)}) async-start(bf16[16,9,8,128]{3,2,1,0:T(8,128)(2,1)} %pad_maximum_fusion), calls=%async_computation.1 | async-start | bytes 589824 | tf_op jit(solution)/shard_map/all_to_all | solution.py:373
  30.6 28.6 %inner.1.rest_4_ = bf16[64,96,768]{2,1,0:T(8,128)(2,1)} custom-call(s32[256]{0:T(256)} %pad_add_fusion.plan, bf16[64,24,128]{2,1,0:T(8,128)(2,1)} %features.3, bf16[896,1536]{1,0:T(8,128)(2,1)} %rest_1_.3, bf16[1536,6144]{1,0:T(8,128)(2,1)} %rest_2_.1, f32[1,5376]{1,0:T(1,128)} %broadcast_in_dim.53.rest_2_.rest_3_), custom_call_target="tpu_custom_call" | custom-call | flops 14495514624 | bytes 26345472 | tf_op jit(solution)/shard_map/inner/pallas_call | solution.py:280
  59.2 0.0 all-to-all-done.1.rest_0_
  59.3 0.0 copy-start
  59.3 0.7 copy-done
  60.0 20.7 %edges.1 = bf16[64,96,768]{2,1,0:T(8,128)(2,1)} custom-call(s32[256]{0:T(256)} %pad_add_fusion.plan, bf16[64,24,128]{2,1,0:T(8,128)(2,1)} %features.3, bf16[16,9,8,128]{3,2,1,0:T(8,128)(2,1)} %copy-done, bf16[896,1536]{1,0:T(8,128)(2,1)} %rest_1_.3, bf16[1536,6144]{1,0:T(8,128)(2,1)} %rest_2_.1, ...), custom_call_target="tpu_custom_call", output_to_operand_aliasing={{}: (6, {})} | custom-call | flops 7247757312 | bytes 23986176 | tf_op jit(solution)/shard_map/edges/pallas_call | solution.py:280
  (14 shorter events, 0.2 us)
Async XLA Ops:
  4.1 17.1 %all-to-all-start = ((bf16[16,5,8,128]{3,2,1,0:T(8,128)(2,1)}), bf16[16,5,8,128]{3,2,1,0:T(8,128)(2,1)S(1)}, u32[]{:S(2)}, u32[]{:S(2)}) async-start(bf16[16,5,8,128]{3,2,1,0:T(8,128)(2,1)} %pad_maximum_fusion.1), calls=%async_computation | async-start | bytes 327680 | tf_op jit(solution)/shard_map/all_to_all | solution.py:371
  14.9 4.0 %collective-permute-start.1 = (bf16[5,8,128]{2,1,0:T(8,128)(2,1)S(1)}, bf16[5,8,128]{2,1,0:T(8,128)(2,1)S(1)}, u32[]{:S(2)}, u32[]{:S(2)}) collective-permute-start(bf16[5,8,128]{2,1,0:T(8,128)(2,1)S(1)} %slice_bitcast_fusion), channel_id=1, source_target_pairs={{0,112},{16,0},{32,16},{48,32},{64,48},{80,64},{96,80},{112,96},{1... | collective-permute-start | bytes 30728 | tf_op jit(solution)/shard_map/ppermute | solution.py:357
  16.8 4.3 %collective-permute-start = (bf16[5,8,128]{2,1,0:T(8,128)(2,1)S(1)}, bf16[5,8,128]{2,1,0:T(8,128)(2,1)S(1)}, u32[]{:S(2)}, u32[]{:S(2)}) collective-permute-start(bf16[5,8,128]{2,1,0:T(8,128)(2,1)S(1)} %slice_bitcast_fusion), channel_id=1, source_target_pairs={{0,16},{16,32},{32,48},{48,64},{64,80},{80,96},{96,112},{112,0},{1... | collective-permute-start | bytes 30728 | tf_op jit(solution)/shard_map/ppermute | solution.py:356
  23.4 35.9 %all-to-all-start.1 = ((bf16[16,9,8,128]{3,2,1,0:T(8,128)(2,1)}), bf16[16,9,8,128]{3,2,1,0:T(8,128)(2,1)S(1)}, u32[]{:S(2)}, u32[]{:S(2)}) async-start(bf16[16,9,8,128]{3,2,1,0:T(8,128)(2,1)} %pad_maximum_fusion), calls=%async_computation.1 | async-start | bytes 589824 | tf_op jit(solution)/shard_map/all_to_all | solution.py:373
  59.3 0.7 copy-start
where the time goes:
time: 81.7 us; the launch traced here: 80.9 us
  Pallas kernels  49.4 us (60%)
  starting transfers between devices  17 us (21%)
  other arithmetic  5.87 us (7%)
  local copies, waits for them, and re-layouts  5.32 us (7%)
  waiting for transfers between devices  2.23 us (3%)
    pallas_call x2, Pallas kernels, vocode(): pl.pallas_call(functools.partial(vocode_kernel, starts, frames, rims), ou...  49.4 us
    all_to_all x1, starting transfers between devices, on_device(): got = lax.all_to_all(rims, 'voc', split_axis=0, concat_axis=0, tiled=True)  7.84 us
    all_to_all x1, starting transfers between devices, on_device(): home = lax.all_to_all(back, 'voc', split_axis=0, concat_axis=0, tiled=True)  7.22 us
    ppermute x1, waiting for transfers between devices, from_groups(): lax.ppermute(own, 'gen', [(g, (g + 1) % count) for g in range(count)])  2.22 us
    ppermute x1, starting transfers between devices, from_groups(): lax.ppermute(own, 'gen', [(g, (g - 1) % count) for g in range(count)])  1.89 us
  transfers between devices with their start and end apart: 4, of which 1 were waited for; matrix products, arithmetic and copies ran while one was open for 6% of the time, Pallas kernels for 35%

commit v1 on v0

--- a/solution.py
+++ b/solution.py
@@ -115,7 +115,7 @@
                         total = total + jnp.where(codes[row + e : row + e + 1] == code, entry, 0.0)
                     return total
 
-                total = lax.fori_loop(0, home.shape[0], look, jnp.zeros((2 * RIM, LANES), jnp.float32), unroll=2)
+                total = lax.fori_loop(0, home.shape[0], look, jnp.zeros((2 * RIM, LANES), jnp.float32), unroll=4)
                 return total[rows_from : rows_from + RIM]
 
             @pl.when(worker == 0)

time: 81.7 us -> 81.3 us (level)
  the two profiles are of different devices: /device:TPU:36 before, /device:TPU:6 now
where the time goes in v1:
time: 81.3 us; the launch traced here: 80.4 us
  Pallas kernels  48.4 us (60%)
  starting transfers between devices  17.4 us (21%)
  other arithmetic  5.87 us (7%)
  local copies, waits for them, and re-layouts  5.32 us (7%)
  waiting for transfers between devices  2.23 us (3%)
    pallas_call x2, Pallas kernels, vocode(): pl.pallas_call(functools.partial(vocode_kernel, starts, frames, rims), ou...  48.4 us
    all_to_all x1, starting transfers between devices, on_device(): got = lax.all_to_all(rims, 'voc', split_axis=0, concat_axis=0, tiled=True)  8.27 us
    all_to_all x1, starting transfers between devices, on_device(): home = lax.all_to_all(back, 'voc', split_axis=0, concat_axis=0, tiled=True)  7.23 us
    ppermute x1, waiting for transfers between devices, from_groups(): lax.ppermute(own, 'gen', [(g, (g + 1) % count) for g in range(count)])  2.22 us
    ppermute x1, starting transfers between devices, from_groups(): lax.ppermute(own, 'gen', [(g, (g - 1) % count) for g in range(count)])  1.89 us
  transfers between devices with their start and end apart: 4, of which 1 were waited for; matrix products, arithmetic and copies ran while one was open for 6% of the time, Pallas kernels for 36%

profile of v1, /device:TPU:6, one launch (start us, length us, event | category | flops | bytes accessed | tf_op | source)
XLA Modules:
  0.0 80.4 jit_solution(706897528876325135)
XLA Ops:
  0.0 0.7 fusion.28
  0.7 0.1 convert_reduce_fusion.2
  0.8 0.7 add_select_fusion
  1.4 0.1 select_reduce_fusion.1
  1.6 0.1 convert_element_type.79
  1.7 0.1 convert_element_type.77
  1.8 1.0 %fusion.29 = (bf16[64,4,128]{2,1,0:T(4,128)(2,1)S(1)}, bf16[64,4,128]{2,1,0:T(4,128)(2,1)S(1)}) fusion(bf16[64,24,128]{2,1,0:T(8,128)(2,1)} %features.3), kind=kLoop, calls=%fused_computation.68 | loop fusion | bytes 262144 | tf_op jit(solution)/shard_map/slice | solution.py:333
  2.8 0.1 convolution_convert_fusion.3
  3.0 0.1 convolution_convert_fusion.2
  3.2 0.1 pad_maximum_fusion.3
  3.2 0.1 broadcast_in_dim.50
  3.3 0.7 pad_maximum_fusion.1
  4.1 8.3 %all-to-all-start = ((bf16[16,5,8,128]{3,2,1,0:T(8,128)(2,1)}), bf16[16,5,8,128]{3,2,1,0:T(8,128)(2,1)S(1)}, u32[]{:S(2)}, u32[]{:S(2)}) async-start(bf16[16,5,8,128]{3,2,1,0:T(8,128)(2,1)} %pad_maximum_fusion.1), calls=%async_computation | async-start | bytes 327680 | tf_op jit(solution)/shard_map/all_to_all | solution.py:371
  12.3 0.7 slice_bitcast_fusion
  13.1 0.8 copy.14
  13.8 0.1 reshape.88
  14.0 1.3 %pad_add_fusion.plan = s32[256]{0:T(256)} fusion(s32[192]{0:T(256)S(1)} %reshape.88, s32[64]{0:T(128)} %param.9), kind=kLoop, calls=%fused_computation.58 | loop fusion | flops 256 | bytes 2048 | tf_op jit(solution)/shard_map/concatenate | solution.py:369
  15.3 1.9 %collective-permute-start.1 = (bf16[5,8,128]{2,1,0:T(8,128)(2,1)S(1)}, bf16[5,8,128]{2,1,0:T(8,128)(2,1)S(1)}, u32[]{:S(2)}, u32[]{:S(2)}) collective-permute-start(bf16[5,8,128]{2,1,0:T(8,128)(2,1)S(1)} %slice_bitcast_fusion), channel_id=1, source_target_pairs={{0,112},{16,0},{32,16},{48,32},{64,48},{80,64},{96,80},{112,96},{1... | collective-permute-start | bytes 30728 | tf_op jit(solution)/shard_map/ppermute | solution.py:357
  17.2 0.0 collective-permute-start
  17.2 0.7 reshape.97
  17.9 0.7 pad_maximum_fusion.2
  18.6 0.6 broadcast_in_dim.53.rest_2_.rest_3_
  19.3 0.0 collective-permute-done.1
  19.3 2.2 %collective-permute-done = bf16[5,8,128]{2,1,0:T(8,128)(2,1)S(1)} collective-permute-done((bf16[5,8,128]{2,1,0:T(8,128)(2,1)S(1)}, bf16[5,8,128]{2,1,0:T(8,128)(2,1)S(1)}, u32[]{:S(2)}, u32[]{:S(2)}) %collective-permute-start) | collective-permute-done | bytes 10272 | tf_op jit(solution)/shard_map/ppermute | solution.py:356
  21.5 0.0 all-to-all-done
  21.6 0.6 convert_reduce_fusion.1
  22.2 0.1 reshape.98
  22.3 0.1 reshape.99
  22.4 0.3 convolution_convert_fusion
  22.7 0.2 convolution_convert_fusion.1
  23.0 0.8 pad_maximum_fusion
  23.8 7.2 %all-to-all-start.1 = ((bf16[16,9,8,128]{3,2,1,0:T(8,128)(2,1)}), bf16[16,9,8,128]{3,2,1,0:T(8,128)(2,1)S(1)}, u32[]{:S(2)}, u32[]{:S(2)}) async-start(bf16[16,9,8,128]{3,2,1,0:T(8,128)(2,1)} %pad_maximum_fusion), calls=%async_computation.1 | async-start | bytes 589824 | tf_op jit(solution)/shard_map/all_to_all | solution.py:373
  31.0 28.9 %inner.1.rest_4_ = bf16[64,96,768]{2,1,0:T(8,128)(2,1)} custom-call(s32[256]{0:T(256)} %pad_add_fusion.plan, bf16[64,24,128]{2,1,0:T(8,128)(2,1)} %features.3, bf16[896,1536]{1,0:T(8,128)(2,1)} %rest_1_.3, bf16[1536,6144]{1,0:T(8,128)(2,1)} %rest_2_.1, f32[1,5376]{1,0:T(1,128)} %broadcast_in_dim.53.rest_2_.rest_3_), custom_call_target="tpu_custom_call" | custom-call | flops 14495514624 | bytes 26345472 | tf_op jit(solution)/shard_map/inner/pallas_call | solution.py:280
  59.9 0.0 all-to-all-done.1.rest_0_
  59.9 0.0 copy-start
  59.9 0.7 copy-done
  60.6 19.6 %edges.1 = bf16[64,96,768]{2,1,0:T(8,128)(2,1)} custom-call(s32[256]{0:T(256)} %pad_add_fusion.plan, bf16[64,24,128]{2,1,0:T(8,128)(2,1)} %features.3, bf16[16,9,8,128]{3,2,1,0:T(8,128)(2,1)} %copy-done, bf16[896,1536]{1,0:T(8,128)(2,1)} %rest_1_.3, bf16[1536,6144]{1,0:T(8,128)(2,1)} %rest_2_.1, ...), custom_call_target="tpu_custom_call", output_to_operand_aliasing={{}: (6, {})} | custom-call | flops 7247757312 | bytes 23986176 | tf_op jit(solution)/shard_map/edges/pallas_call | solution.py:280
  (14 shorter events, 0.2 us)
Async XLA Ops:
  4.1 17.5 %all-to-all-start = ((bf16[16,5,8,128]{3,2,1,0:T(8,128)(2,1)}), bf16[16,5,8,128]{3,2,1,0:T(8,128)(2,1)S(1)}, u32[]{:S(2)}, u32[]{:S(2)}) async-start(bf16[16,5,8,128]{3,2,1,0:T(8,128)(2,1)} %pad_maximum_fusion.1), calls=%async_computation | async-start | bytes 327680 | tf_op jit(solution)/shard_map/all_to_all | solution.py:371
  15.3 4.0 %collective-permute-start.1 = (bf16[5,8,128]{2,1,0:T(8,128)(2,1)S(1)}, bf16[5,8,128]{2,1,0:T(8,128)(2,1)S(1)}, u32[]{:S(2)}, u32[]{:S(2)}) collective-permute-start(bf16[5,8,128]{2,1,0:T(8,128)(2,1)S(1)} %slice_bitcast_fusion), channel_id=1, source_target_pairs={{0,112},{16,0},{32,16},{48,32},{64,48},{80,64},{96,80},{112,96},{1... | collective-permute-start | bytes 30728 | tf_op jit(solution)/shard_map/ppermute | solution.py:357
  17.2 4.3 %collective-permute-start = (bf16[5,8,128]{2,1,0:T(8,128)(2,1)S(1)}, bf16[5,8,128]{2,1,0:T(8,128)(2,1)S(1)}, u32[]{:S(2)}, u32[]{:S(2)}) collective-permute-start(bf16[5,8,128]{2,1,0:T(8,128)(2,1)S(1)} %slice_bitcast_fusion), channel_id=1, source_target_pairs={{0,16},{16,32},{32,48},{48,64},{64,80},{80,96},{96,112},{112,0},{1... | collective-permute-start | bytes 30728 | tf_op jit(solution)/shard_map/ppermute | solution.py:356
  23.8 36.1 %all-to-all-start.1 = ((bf16[16,9,8,128]{3,2,1,0:T(8,128)(2,1)}), bf16[16,9,8,128]{3,2,1,0:T(8,128)(2,1)S(1)}, u32[]{:S(2)}, u32[]{:S(2)}) async-start(bf16[16,9,8,128]{3,2,1,0:T(8,128)(2,1)} %pad_maximum_fusion), calls=%async_computation.1 | async-start | bytes 589824 | tf_op jit(solution)/shard_map/all_to_all | solution.py:373
  59.9 0.7 copy-start

commit v2 on v1

--- a/solution.py
+++ b/solution.py
@@ -115,7 +115,7 @@
                         total = total + jnp.where(codes[row + e : row + e + 1] == code, entry, 0.0)
                     return total
 
-                total = lax.fori_loop(0, home.shape[0], look, jnp.zeros((2 * RIM, LANES), jnp.float32), unroll=4)
+                total = lax.fori_loop(0, home.shape[0], look, jnp.zeros((2 * RIM, LANES), jnp.float32), unroll=8)
                 return total[rows_from : rows_from + RIM]
 
             @pl.when(worker == 0)

time: 81.3 us -> 81.1 us (level)
  the two profiles are of different devices: /device:TPU:6 before, /device:TPU:0 now
where the time goes in v2:
time: 81.1 us; the launch traced here: 80.3 us
  Pallas kernels  48.7 us (60%)
  starting transfers between devices  17.1 us (21%)
  other arithmetic  5.87 us (7%)
  local copies, waits for them, and re-layouts  5.29 us (7%)
  waiting for transfers between devices  2.23 us (3%)
    pallas_call x2, Pallas kernels, vocode(): pl.pallas_call(functools.partial(vocode_kernel, starts, frames, rims), ou...  48.7 us
    all_to_all x1, starting transfers between devices, on_device(): got = lax.all_to_all(rims, 'voc', split_axis=0, concat_axis=0, tiled=True)  7.96 us
    all_to_all x1, starting transfers between devices, on_device(): home = lax.all_to_all(back, 'voc', split_axis=0, concat_axis=0, tiled=True)  6.96 us
    ppermute x1, waiting for transfers between devices, from_groups(): lax.ppermute(own, 'gen', [(g, (g + 1) % count) for g in range(count)])  2.22 us
    ppermute x1, starting transfers between devices, from_groups(): lax.ppermute(own, 'gen', [(g, (g - 1) % count) for g in range(count)])  2.17 us
  transfers between devices with their start and end apart: 4, of which 1 were waited for; matrix products, arithmetic and copies ran while one was open for 6% of the time, Pallas kernels for 36%

profile of v2, /device:TPU:0, one launch (start us, length us, event | category | flops | bytes accessed | tf_op | source)
XLA Modules:
  0.0 80.3 jit_solution(15845754967399262830)
XLA Ops:
  0.0 0.7 fusion.28
  0.7 0.1 convert_reduce_fusion.2
  0.8 0.7 add_select_fusion
  1.4 0.1 select_reduce_fusion.1
  1.6 0.1 convert_element_type.79
  1.7 0.1 convert_element_type.77
  1.8 1.0 %fusion.29 = (bf16[64,4,128]{2,1,0:T(4,128)(2,1)S(1)}, bf16[64,4,128]{2,1,0:T(4,128)(2,1)S(1)}) fusion(bf16[64,24,128]{2,1,0:T(8,128)(2,1)} %features.3), kind=kLoop, calls=%fused_computation.68 | loop fusion | bytes 262144 | tf_op jit(solution)/shard_map/slice | solution.py:333
  2.8 0.1 convolution_convert_fusion.3
  3.0 0.1 convolution_convert_fusion.2
  3.2 0.1 pad_maximum_fusion.3
  3.2 0.1 broadcast_in_dim.50
  3.3 0.7 pad_maximum_fusion.1
  4.1 8.0 %all-to-all-start = ((bf16[16,5,8,128]{3,2,1,0:T(8,128)(2,1)}), bf16[16,5,8,128]{3,2,1,0:T(8,128)(2,1)S(1)}, u32[]{:S(2)}, u32[]{:S(2)}) async-start(bf16[16,5,8,128]{3,2,1,0:T(8,128)(2,1)} %pad_maximum_fusion.1), calls=%async_computation | async-start | bytes 327680 | tf_op jit(solution)/shard_map/all_to_all | solution.py:371
  12.0 0.7 slice_bitcast_fusion
  12.7 0.8 copy.14
  13.5 0.1 reshape.88
  13.7 1.3 %pad_add_fusion.plan = s32[256]{0:T(256)} fusion(s32[192]{0:T(256)S(1)} %reshape.88, s32[64]{0:T(128)} %param.9), kind=kLoop, calls=%fused_computation.58 | loop fusion | flops 256 | bytes 2048 | tf_op jit(solution)/shard_map/concatenate | solution.py:369
  15.0 2.2 %collective-permute-start.1 = (bf16[5,8,128]{2,1,0:T(8,128)(2,1)S(1)}, bf16[5,8,128]{2,1,0:T(8,128)(2,1)S(1)}, u32[]{:S(2)}, u32[]{:S(2)}) collective-permute-start(bf16[5,8,128]{2,1,0:T(8,128)(2,1)S(1)} %slice_bitcast_fusion), channel_id=1, source_target_pairs={{0,112},{16,0},{32,16},{48,32},{64,48},{80,64},{96,80},{112,96},{1... | collective-permute-start | bytes 30728 | tf_op jit(solution)/shard_map/ppermute | solution.py:357
  17.1 0.0 collective-permute-start
  17.2 0.7 reshape.97
  17.9 0.7 pad_maximum_fusion.2
  18.6 0.6 broadcast_in_dim.53.rest_2_.rest_3_
  19.2 0.0 collective-permute-done.1
  19.2 2.2 %collective-permute-done = bf16[5,8,128]{2,1,0:T(8,128)(2,1)S(1)} collective-permute-done((bf16[5,8,128]{2,1,0:T(8,128)(2,1)S(1)}, bf16[5,8,128]{2,1,0:T(8,128)(2,1)S(1)}, u32[]{:S(2)}, u32[]{:S(2)}) %collective-permute-start) | collective-permute-done | bytes 10272 | tf_op jit(solution)/shard_map/ppermute | solution.py:356
  21.5 0.0 all-to-all-done
  21.5 0.6 convert_reduce_fusion.1
  22.1 0.1 reshape.98
  22.2 0.1 reshape.99
  22.4 0.3 convolution_convert_fusion
  22.7 0.2 convolution_convert_fusion.1
  23.0 0.8 pad_maximum_fusion
  23.8 7.0 %all-to-all-start.1 = ((bf16[16,9,8,128]{3,2,1,0:T(8,128)(2,1)}), bf16[16,9,8,128]{3,2,1,0:T(8,128)(2,1)S(1)}, u32[]{:S(2)}, u32[]{:S(2)}) async-start(bf16[16,9,8,128]{3,2,1,0:T(8,128)(2,1)} %pad_maximum_fusion), calls=%async_computation.1 | async-start | bytes 589824 | tf_op jit(solution)/shard_map/all_to_all | solution.py:373
  30.7 28.6 %inner.1.rest_4_ = bf16[64,96,768]{2,1,0:T(8,128)(2,1)} custom-call(s32[256]{0:T(256)} %pad_add_fusion.plan, bf16[64,24,128]{2,1,0:T(8,128)(2,1)} %features.3, bf16[896,1536]{1,0:T(8,128)(2,1)} %rest_1_.3, bf16[1536,6144]{1,0:T(8,128)(2,1)} %rest_2_.1, f32[1,5376]{1,0:T(1,128)} %broadcast_in_dim.53.rest_2_.rest_3_), custom_call_target="tpu_custom_call" | custom-call | flops 14495514624 | bytes 26345472 | tf_op jit(solution)/shard_map/inner/pallas_call | solution.py:280
  59.3 0.0 all-to-all-done.1.rest_0_
  59.3 0.0 copy-start
  59.3 0.7 copy-done
  60.0 20.1 %edges.1 = bf16[64,96,768]{2,1,0:T(8,128)(2,1)} custom-call(s32[256]{0:T(256)} %pad_add_fusion.plan, bf16[64,24,128]{2,1,0:T(8,128)(2,1)} %features.3, bf16[16,9,8,128]{3,2,1,0:T(8,128)(2,1)} %copy-done, bf16[896,1536]{1,0:T(8,128)(2,1)} %rest_1_.3, bf16[1536,6144]{1,0:T(8,128)(2,1)} %rest_2_.1, ...), custom_call_target="tpu_custom_call", output_to_operand_aliasing={{}: (6, {})} | custom-call | flops 7247757312 | bytes 23986176 | tf_op jit(solution)/shard_map/edges/pallas_call | solution.py:280
  (14 shorter events, 0.2 us)
Async XLA Ops:
  4.1 17.4 %all-to-all-start = ((bf16[16,5,8,128]{3,2,1,0:T(8,128)(2,1)}), bf16[16,5,8,128]{3,2,1,0:T(8,128)(2,1)S(1)}, u32[]{:S(2)}, u32[]{:S(2)}) async-start(bf16[16,5,8,128]{3,2,1,0:T(8,128)(2,1)} %pad_maximum_fusion.1), calls=%async_computation | async-start | bytes 327680 | tf_op jit(solution)/shard_map/all_to_all | solution.py:371
  15.0 4.2 %collective-permute-start.1 = (bf16[5,8,128]{2,1,0:T(8,128)(2,1)S(1)}, bf16[5,8,128]{2,1,0:T(8,128)(2,1)S(1)}, u32[]{:S(2)}, u32[]{:S(2)}) collective-permute-start(bf16[5,8,128]{2,1,0:T(8,128)(2,1)S(1)} %slice_bitcast_fusion), channel_id=1, source_target_pairs={{0,112},{16,0},{32,16},{48,32},{64,48},{80,64},{96,80},{112,96},{1... | collective-permute-start | bytes 30728 | tf_op jit(solution)/shard_map/ppermute | solution.py:357
  17.1 4.3 %collective-permute-start = (bf16[5,8,128]{2,1,0:T(8,128)(2,1)S(1)}, bf16[5,8,128]{2,1,0:T(8,128)(2,1)S(1)}, u32[]{:S(2)}, u32[]{:S(2)}) collective-permute-start(bf16[5,8,128]{2,1,0:T(8,128)(2,1)S(1)} %slice_bitcast_fusion), channel_id=1, source_target_pairs={{0,16},{16,32},{32,48},{48,64},{64,80},{80,96},{96,112},{112,0},{1... | collective-permute-start | bytes 30728 | tf_op jit(solution)/shard_map/ppermute | solution.py:356
  23.8 35.6 %all-to-all-start.1 = ((bf16[16,9,8,128]{3,2,1,0:T(8,128)(2,1)}), bf16[16,9,8,128]{3,2,1,0:T(8,128)(2,1)S(1)}, u32[]{:S(2)}, u32[]{:S(2)}) async-start(bf16[16,9,8,128]{3,2,1,0:T(8,128)(2,1)} %pad_maximum_fusion), calls=%async_computation.1 | async-start | bytes 589824 | tf_op jit(solution)/shard_map/all_to_all | solution.py:373
  59.3 0.7 copy-start
